TPU v7x, 256 devices: a whole 4x4x8 slice. The times are simulated.
256 devices in a mesh: rep: 16 (over z, core), fsdp: 16 (over y, x).
Axes of the slice: x: 4, y: 4, z: 8, core: 2. Of those that a mesh axis runs over, the one named last changes fastest.
Arguments:
- gradients: bfloat16 [16, 4, 1024, 8192], P('rep', None, None, 'fsdp'), may hold values from -12 to 12
- old_left: float32 [64, 1024, 1024], P('fsdp', 'rep'), may hold values from -6 to 6
- old_right: float32 [64, 1024, 1024], P('fsdp', 'rep'), may hold values from -6 to 6
- left_root: float32 [64, 1024, 1024], P('fsdp', 'rep'), may hold values from -20 to 20, as said below
- right_root: float32 [64, 1024, 1024], P('fsdp', 'rep'), may hold values from -20 to 20, as said below
- owner_plan: int32 [4, 8], replicated, may hold values from 0 to 15, as said below
Outputs:
- new_left: float32 [64, 1024, 1024], P('fsdp', 'rep')
- new_right: float32 [64, 1024, 1024], P('fsdp', 'rep')
- direction: bfloat16 [4, 1024, 8192], P(None, 'rep', 'fsdp')
Inputs may be any that keep to these rules, and one draw needn't show every extreme that they name: `owner_plan`: no fsdp index owns more than 4 blocks, and some index owns exactly 4. `left_root`: every one of the 64 blocks is symmetric. `right_root`: every one of the 64 blocks is symmetric.
All inputs are finite; a program needn't handle non-finite values.
Results may differ from a plain program's by a relative error of at most 0.025.
Values may be sent and summed in bfloat16 or wider, within the bound.
A program may use at most 128 MiB of HBM per device.

v0:
```python
import jax
import jax.numpy as jnp
from jax import lax
from jax.sharding import PartitionSpec as P

gram_decay = 0.95


def ownership(owner_plan):
    owners = owner_plan.reshape(-1)
    positions = jnp.arange(owners.shape[0], dtype=jnp.int32)
    earlier = (owners[:, None] == owners[None, :]) & (positions[None, :] < positions[:, None])
    return (owners, jnp.sum(earlier.astype(jnp.int32), axis=1))


def local(gradients, old_left, old_right, left_root, right_root, owner_plan):
    rep_count = lax.axis_size("rep")
    my_index = lax.axis_index("fsdp")
    rep_index = lax.axis_index("rep")
    local_grad = gradients[0]
    layer_count, kv_width, home_cols = local_grad.shape
    slot_count, rows_rep, block_size = old_left.shape
    per_layer = owner_plan.shape[1]
    owners, slot_of = ownership(owner_plan)
    block_count = owners.shape[0]
    summed = lax.psum_scatter(
        local_grad.astype(jnp.float32).astype(jnp.bfloat16), "rep", scatter_dimension=1, tiled=True
    ).astype(jnp.float32)
    reduced = (summed / rep_count).astype(jnp.bfloat16)
    row_slices = lax.all_gather(reduced, "fsdp", axis=2, tiled=True)
    slot_ids = jnp.arange(slot_count, dtype=jnp.int32)
    block_ids = jnp.arange(block_count, dtype=jnp.int32)
    held_slot = (owners[None, :] == my_index) & (slot_of[None, :] == slot_ids[:, None])
    is_live = jnp.any(held_slot, axis=1)
    chosen = jnp.sum(jnp.where(held_slot, block_ids[None, :], 0), axis=1)

    def take_block(block_id):
        return lax.dynamic_slice(
            row_slices,
            (block_id // per_layer, 0, block_id % per_layer * block_size),
            (1, rows_rep, block_size),
        )[0]

    pieces = jax.vmap(take_block)(chosen)
    pieces = jnp.where(is_live[:, None, None], pieces, jnp.zeros_like(pieces))
    full_block = lax.all_gather(pieces, "rep", axis=1, tiled=True)
    gram_left = jnp.einsum("spk,sqk->spq", pieces, full_block, preferred_element_type=jnp.float32)
    columns = lax.dynamic_slice_in_dim(full_block, rep_index * rows_rep, rows_rep, 2)
    gram_right = jnp.einsum("sic,sij->scj", columns, full_block, preferred_element_type=jnp.float32)
    new_left = gram_decay * old_left + (1.0 - gram_decay) * gram_left
    new_right = gram_decay * old_right + (1.0 - gram_decay) * gram_right
    transposed = jnp.einsum(
        "sck,sik->sci",
        right_root,
        full_block,
        precision=lax.Precision.HIGHEST,
        preferred_element_type=jnp.float32,
    ).astype(jnp.bfloat16)
    directions = jnp.einsum(
        "sri,sci->src",
        left_root,
        lax.all_gather(transposed, "rep", axis=1, tiled=True),
        precision=lax.Precision.HIGHEST,
        preferred_element_type=jnp.float32,
    ).astype(jnp.bfloat16)
    piece_cols = min(home_cols, block_size)
    home_pieces = home_cols // piece_cols
    item_ids = jnp.arange(layer_count * home_pieces, dtype=jnp.int32)
    layer_id = item_ids // home_pieces
    start_col = my_index * home_cols + item_ids % home_pieces * piece_cols
    wanted_block = layer_id * per_layer + start_col // block_size
    within = start_col % block_size
    everything = lax.all_gather(directions, "fsdp", axis=0, tiled=True)
    source_slot = owners[wanted_block] * slot_count + slot_of[wanted_block]

    def cut_piece(slot_pick, col_offset):
        return lax.dynamic_slice(everything, (slot_pick, 0, col_offset), (1, rows_rep, piece_cols))[
            0
        ]

    received_parts = jax.vmap(cut_piece)(source_slot, within)
    direction = received_parts.reshape(layer_count, home_pieces, rows_rep, piece_cols).transpose(
        0, 2, 1, 3
    )
    direction = direction.reshape(layer_count, rows_rep, home_cols)
    return (new_left, new_right, direction)


def solution(mesh):
    return jax.shard_map(
        local,
        mesh=mesh,
        in_specs=(
            P("rep", None, None, "fsdp"),
            P("fsdp", "rep", None),
            P("fsdp", "rep", None),
            P("fsdp", "rep", None),
            P("fsdp", "rep", None),
            P(),
        ),
        out_specs=(P("fsdp", "rep", None), P("fsdp", "rep", None), P(None, "rep", "fsdp")),
        check_vma=False,
    )
```

profile of v0, /device:TPU:1, one launch (start us, length us, event | category | flops | bytes accessed | tf_op | source)
XLA Modules:
  0.0 395.0 jit_solution(14453118954260329591)
XLA Ops:
  7.2 0.7 reduce-scatter.2.cloned.1.call-update
  8.0 66.1 %reduce-scatter.2.cloned.1.call-done = bf16[4,64,512]{2,1,0:T(8,128)(2,1)} async-done(((bf16[4,1024,512]{2,1,0:T(8,128)(2,1)}), bf16[4,64,512]{2,1,0:T(8,128)(2,1)}) %reduce-scatter.2.cloned.1.call-update) | async-done | bytes 262160 | tf_op jit(solution)/shard_map/reduce_scatter | solution.py:26
  74.0 1.7 multiply_convert_fusion
  75.8 0.0 all-gather.7.cloned.1.call-start
  75.8 0.8 broadcast_in_dim_reshape.2
  76.6 0.2 convert_reduce_fusion
  76.8 0.1 select_reduce_fusion
  77.0 0.1 copy.21
  77.0 0.1 fusion.7
  77.2 63.2 %all-gather.5.cloned.1.call-done = bf16[4,64,8192]{2,1,0:T(8,128)(2,1)} async-done(((bf16[4,64,512]{2,1,0:T(8,128)(2,1)}), bf16[4,64,8192]{2,1,0:T(8,128)(2,1)}) %all-gather.5.cloned.1.call-update) | async-done | bytes 4194320 | tf_op jit(solution)/shard_map/all_gather | solution.py:30
  140.4 11.7 %while.1 = (s32[]{:T(128)}, bf16[4,64,8192]{2,1,0:T(8,128)(2,1)}, s32[4,3]{1,0:T(4,128)S(1)}, bf16[4,1,64,1024]{3,2,1,0:T(8,128)(2,1)S(1)}, s32[]{:T(128)}) while((s32[]{:T(128)}, bf16[4,64,8192]{2,1,0:T(8,128)(2,1)}, s32[4,3]{1,0:T(4,128)S(1)}, bf16[4,1,64,1024]{3,2,1,0:T(8,128)(2,1)S(1)}, s32[]{:T(128)}) %tuple.32), condition=%wide.while_cond, body=%wide.while_body.sunk | while | flops 2 | bytes 262269 | solution.py:38
  140.4 0.6 fusion.24
  141.0 2.3 bitcast_dynamic-update-slice_fusion.2
  143.3 0.6 fusion.24
  143.9 2.3 bitcast_dynamic-update-slice_fusion.2
  146.3 0.6 fusion.24
  146.9 2.3 bitcast_dynamic-update-slice_fusion.2
  149.2 0.6 fusion.24
  149.8 2.3 bitcast_dynamic-update-slice_fusion.2
  152.1 0.9 bitcast_select_fusion
  153.1 56.7 %all-gather.7.cloned.1.call-done = bf16[4,1024,1024]{2,1,0:T(8,128)(2,1)} async-done(((bf16[4,64,1024]{2,1,0:T(8,128)(2,1)}), bf16[4,1024,1024]{2,1,0:T(8,128)(2,1)}) %all-gather.7.cloned.1.call-update) | async-done | bytes 8388624 | tf_op jit(solution)/shard_map/all_gather | solution.py:46
  209.8 10.8 %fusion.2 = bf16[4,64,1024]{2,1,0:T(8,128)(2,1)} fusion(bf16[4,1024,1024]{2,1,0:T(8,128)(2,1)} %all-gather.7.cloned.1.call-done, f32[4,64,1024]{2,1,0:T(8,128)S(1)} %copy-done), kind=kOutput, calls=%fused_computation.11 | convolution fusion | flops 3221487616 | bytes 9961472 | tf_op jit(solution)/shard_map/sck,sik->sci/dot_general | solution.py:52
  220.7 54.6 %all-gather.9.cloned.1.call-done = bf16[4,1024,1024]{2,1,0:T(8,128)(2,1)} async-done(((bf16[4,64,1024]{2,1,0:T(8,128)(2,1)}), bf16[4,1024,1024]{2,1,0:T(8,128)(2,1)}) %all-gather.9.cloned.1.call-update) | async-done | bytes 8388624 | tf_op jit(solution)/shard_map/all_gather | solution.py:62
  275.3 10.8 %fusion.3 = bf16[4,64,1024]{2,1,0:T(8,128)(2,1)} fusion(bf16[4,1024,1024]{2,1,0:T(8,128)(2,1)} %all-gather.9.cloned.1.call-done, f32[4,64,1024]{2,1,0:T(8,128)S(1)} %copy-done.2), kind=kOutput, calls=%fused_computation.12 | convolution fusion | flops 3221487616 | bytes 9961472 | tf_op jit(solution)/shard_map/sri,sci->src/dot_general | solution.py:59
  286.2 0.6 gather_fusion.1
  286.8 0.6 gather_fusion
  287.5 6.8 %fusion.1 = f32[4,64,1024]{2,1,0:T(8,128)} fusion(bf16[4,1024,1024]{2,1,0:T(8,128)(2,1)} %all-gather.7.cloned.1.call-done, s32[]{:T(128)S(6)} %select_n.115, f32[4,64,1024]{2,1,0:T(8,128)S(1)} %copy-done.3), kind=kOutput, calls=%fused_computation.8 | convolution fusion | flops 537657344 | bytes 11534340 | tf_op jit(solution)/shard_map/sic,sij->scj/dot_general | solution.py:49
  294.3 7.4 %fusion = f32[4,64,1024]{2,1,0:T(8,128)} fusion(bf16[4,64,1024]{2,1,0:T(8,128)(2,1)S(1)} %copy-done.1, bf16[4,1024,1024]{2,1,0:T(8,128)(2,1)} %all-gather.7.cloned.1.call-done, f32[4,64,1024]{2,1,0:T(8,128)S(1)} %copy-done.4), kind=kOutput, calls=%fused_computation.6 | convolution fusion | flops 537657344 | bytes 11010048 | tf_op jit(solution)/shard_map/spk,sqk->spq/dot_general | solution.py:47
  301.7 58.7 %all-gather.11.cloned.1.call-done = bf16[64,64,1024]{2,1,0:T(8,128)(2,1)} async-done(((bf16[4,64,1024]{2,1,0:T(8,128)(2,1)}), bf16[64,64,1024]{2,1,0:T(8,128)(2,1)}) %all-gather.11.cloned.1.call-update) | async-done | bytes 8388624 | tf_op jit(solution)/shard_map/all_gather | solution.py:73
  360.4 23.9 %copy.23 = bf16[64,64,1024]{1,0,2:T(8,128)(2,1)} copy(bf16[64,64,1024]{2,1,0:T(8,128)(2,1)} %all-gather.11.cloned.1.call-done) | data formatting | bytes 16777216 | tf_op jit(solution)/shard_map/all_gather | solution.py:73
  384.3 3.1 gather_fusion.2
  387.4 1.0 copy.24
  (30 shorter events, 0.3 us)
Async XLA Ops:
  7.2 202.7 %copy-start = (f32[4,64,1024]{2,1,0:T(8,128)S(1)}, f32[4,64,1024]{2,1,0:T(8,128)}, u32[]{:S(2)}) copy-start(f32[4,64,1024]{2,1,0:T(8,128)} %param.10) | copy-start | bytes 3145732
  7.2 66.9 %reduce-scatter.2.cloned.1.call-start = ((), (), s32[]{:S(2)}) async-start(), calls=%async_computation.1 | async-start | bytes 4456448 | tf_op jit(solution)/shard_map/reduce_scatter | solution.py:26
  7.2 268.1 %copy-start.2 = (f32[4,64,1024]{2,1,0:T(8,128)S(1)}, f32[4,64,1024]{2,1,0:T(8,128)}, u32[]{:S(2)}) copy-start(f32[4,64,1024]{2,1,0:T(8,128)} %param.9) | copy-start | bytes 3145732
  7.9 132.5 %all-gather.5.cloned.1.call-start = ((), (), s32[]{:S(2)}) async-start(), calls=%async_computation.2 | async-start | bytes 4456448 | tf_op jit(solution)/shard_map/all_gather | solution.py:30
  75.8 134.1 %all-gather.7.cloned.1.call-start = ((), (), s32[]{:S(2)}) async-start(), calls=%async_computation.3 | async-start | bytes 8912896 | tf_op jit(solution)/shard_map/all_gather | solution.py:46
  153.0 122.3 %all-gather.9.cloned.1.call-start = ((), (), s32[]{:S(2)}) async-start(), calls=%async_computation.4 | async-start | bytes 8912896 | tf_op jit(solution)/shard_map/all_gather | solution.py:62
  220.6 66.9 %copy-start.3 = (f32[4,64,1024]{2,1,0:T(8,128)S(1)}, f32[4,64,1024]{2,1,0:T(8,128)}, u32[]{:S(2)}) copy-start(f32[4,64,1024]{2,1,0:T(8,128)} %param.8) | copy-start | bytes 3145732
  220.7 139.7 %all-gather.11.cloned.1.call-start = ((), (), s32[]{:S(2)}) async-start(), calls=%async_computation.5 | async-start | bytes 8912896 | tf_op jit(solution)/shard_map/all_gather | solution.py:73
  286.1 8.2 %copy-start.1 = (bf16[4,64,1024]{2,1,0:T(8,128)(2,1)S(1)}, bf16[4,64,1024]{2,1,0:T(8,128)(2,1)}, u32[]{:S(2)}) copy-start(bf16[4,64,1024]{2,1,0:T(8,128)(2,1)} %bitcast_select_fusion) | copy-start | bytes 1572868
  287.5 6.9 %copy-start.4 = (f32[4,64,1024]{2,1,0:T(8,128)S(1)}, f32[4,64,1024]{2,1,0:T(8,128)}, u32[]{:S(2)}) copy-start(f32[4,64,1024]{2,1,0:T(8,128)} %param.7) | copy-start | bytes 3145732
Sparse Core Ops, SparseCore 0:
  10.6 63.4 reduce-scatter.1
  77.0 63.3 all-gather.4
  153.2 56.6 all-gather.6
  220.8 54.4 all-gather.8
  286.3 74.0 all-gather.10
where the time goes:
time: 396 us; the launch traced here: 395 us
  waiting for transfers between devices  300 us (76%)
  local copies, waits for them, and re-layouts  41.8 us (11%)
  matrix products  35.8 us (9%)
  between operations  13.9 us (4%)
    reduce_scatter x1, waiting for transfers between devices, local(): lax.psum_scatter(local_grad.astype(jnp.float32).astype(jnp.bfloat16), 're...  66.1 us
    all_gather x1, waiting for transfers between devices, local(): row_slices = lax.all_gather(reduced, 'fsdp', axis=2, tiled=True)  63.2 us
    all_gather x1, waiting for transfers between devices, local(): everything = lax.all_gather(directions, 'fsdp', axis=0, tiled=True)  58.7 us
    all_gather x1, waiting for transfers between devices, local(): full_block = lax.all_gather(pieces, 'rep', axis=1, tiled=True)  56.7 us
    all_gather x1, waiting for transfers between devices, local(): lax.all_gather(transposed, 'rep', axis=1, tiled=True)  54.6 us
    all_gather x1, local copies, waits for them, and re-layouts, local(): everything = lax.all_gather(directions, 'fsdp', axis=0, tiled=True)  23.9 us
    gather x12, local copies, waits for them, and re-layouts  11.6 us
    dot_general x1, matrix products, local(): jnp.einsum('sri,sci->src', left_root, lax.all_gather(transposed, 'rep', a...  10.8 us
  transfers between devices with their start and end apart: 5, of which 5 were waited for; matrix products, arithmetic and copies ran while one was open for 4% of the time, Pallas kernels for 0%

commit v1 on v0

v1 whole, which is shorter than its diff:
```python
import functools

import jax
import jax.numpy as jnp
from jax import lax
from jax.experimental import pallas as pl
from jax.experimental.pallas import tpu as pltpu
from jax.sharding import PartitionSpec as P

gram_decay = 0.95
MESH = pl.DeviceIdType.MESH
F32 = jnp.float32
BF16 = jnp.bfloat16


class Dims:
    def __init__(self, rep, fsdp, layers, rows, home, slots):
        self.NR, self.NF, self.NZ = rep, fsdp, rep // 2
        self.FX = 4 if fsdp == 16 else 2
        self.FY = fsdp // self.FX
        self.H = self.NZ // 2
        self.STEPS = 2 * self.H - 1
        self.BLK = rows
        self.SR = rows // rep
        self.HC = home
        self.CH = home // 2
        self.SLOTS = slots
        self.CG = 4 if fsdp == 16 else 2
        self.RG = fsdp // self.CG
        self.PR, self.PC = self.SR // self.RG, rows // self.CG


def kernel(
    d,
    grad,
    old_left,
    old_right,
    left_root,
    right_root,
    owner_plan,
    new_left,
    new_right,
    dir_out,
    plan,
    tab_v,
    tab,
    own,
    sib,
    rs_send,
    rs_recv,
    total,
    roots,
    olds,
    send_a,
    recv_a,
    swap_b,
    send_b,
    recv_b,
    Lp,
    Rs,
    Gb,
    Rb,
    g_s,
    left_sum,
    T_s,
    D_s,
    swap_c,
    send_c,
    recv_c0,
    recv_c1,
    send_d,
    recv_d,
    Db,
    own_sem,
    root_sem,
    old_sem,
    plan_sem,
    tab_sem,
    sib_ss,
    sib_rs,
    rs_ss,
    rs_rs,
    aa_ss,
    aa_rs,
    sw_ss,
    sw_rs,
    ex_ss,
    ex_rs,
    ag_ss,
    ag_rs,
):
    NZ, H, NF, FX, FY, STEPS = d.NZ, d.H, d.NF, d.FX, d.FY, d.STEPS
    r, f = lax.axis_index("rep"), lax.axis_index("fsdp")
    z, c = lax.div(r, 2), lax.rem(r, 2)
    y, x = lax.div(f, FX), lax.rem(f, FX)
    q = lax.rem(f, 2)
    up, down = lax.rem(z + 1, NZ) * 2 + c, lax.rem(z + NZ - 1, NZ) * 2 + c
    sibling = z * 2 + 1 - c
    partner = f + 1 - 2 * q

    around = [lax.rem(z + k, NZ) for k in range(NZ)]

    def zat(dist):
        return around[dist % NZ]

    def remote(src, dst, ss, rs, **where):
        return pltpu.make_async_remote_copy(
            src_ref=src, dst_ref=dst, send_sem=ss, recv_sem=rs, device_id=where, device_id_type=MESH
        )

    order = [H]
    for k in range(H - 1, 0, -1):
        order += [k, NZ - k]
    order += [0]

    def own_copy(k):
        return pltpu.make_async_copy(grad.at[:, c, zat(k)], own.at[k], own_sem.at[k])

    def root_copy(m):
        return pltpu.make_async_copy((left_root, right_root)[m], roots.at[m], root_sem.at[m])

    def old_copy(m, s):
        return pltpu.make_async_copy((old_left, old_right)[m].at[s], olds.at[m, s], old_sem.at[m, s])

    plan_copy = pltpu.make_async_copy(owner_plan, plan, plan_sem)
    tab_copy = pltpu.make_async_copy(tab_v, tab, tab_sem)

    barrier = pltpu.get_barrier_semaphore()

    ys = [lax.rem(y + k, FY) * FX for k in range(FY)]
    xs = [lax.rem(x + k, FX) for k in range(FX)]
    peers = [ys[i // FX] + xs[i % FX] for i in range(1, NF)]
    for where in ({"rep": sibling}, {"rep": up}, {"rep": down}, {"rep": sibling, "fsdp": partner}):
        pl.semaphore_signal(barrier, inc=1, device_id=where, device_id_type=MESH)
    for peer in peers:
        pl.semaphore_signal(barrier, inc=1, device_id={"fsdp": peer}, device_id_type=MESH)
    for k in order:
        own_copy(k).start()
    for m in range(2):
        root_copy(m).start()
    plan_copy.start()
    pl.semaphore_wait(barrier, NF - 1 + 4)

    def cut(value, piece):
        rg, cg = piece // d.CG, piece % d.CG
        return value[rg * d.PR : (rg + 1) * d.PR, cg * d.PC : (cg + 1) * d.PC]

    def cast_root(m):
        root_copy(m).wait()

        def go(s, carry):
            value = roots[m, s].astype(BF16)
            for piece in range(NF):
                send_a[piece * d.SLOTS + s, m] = cut(value, piece)
            return carry

        lax.fori_loop(0, d.SLOTS, go, 0)

    layers, columns = plan.shape
    blocks = layers * columns

    def tables():
        plan_copy.wait()
        owner = [plan[b // columns, b % columns] for b in range(blocks)]
        row = lax.broadcasted_iota(jnp.int32, (blocks, 128), 0)
        lane = lax.broadcasted_iota(jnp.int32, (blocks, 128), 1)
        owners = jnp.zeros((blocks, 128), jnp.int32)
        for b in range(blocks):
            owners = jnp.where(row == b, owner[b], owners)
        index = owners * d.SLOTS
        for b in range(blocks - 1):
            index = index + jnp.where((row > b) & (owners == owner[b]), 1, 0)
        places = jnp.zeros((blocks, 128), jnp.int32)
        for b in range(blocks):
            l, j = b // columns, b % columns
            places = jnp.where(row == b, (2 * j + l // 2) * 2 + l % 2, places)
        held = jnp.max(jnp.where(index == lane, places, -1), axis=0, keepdims=True)
        tab_v[0:blocks] = index
        tab_v[blocks : blocks + 8] = jnp.broadcast_to(held, (8, 128))
        tab_copy.start()

    def sib_copy(i, k):
        return remote(
            grad.at[:, 1 - c, zat(k), :, pl.ds(i * d.CH, d.CH)],
            sib.at[i, k],
            sib_ss.at[i],
            sib_rs.at[i, k],
            rep=sibling,
        )

    def rs_items(stream):
        items = [(H, stream)]
        for k in range(H - 1, 0, -1):
            items += [(k, 1 - stream), (k, stream)]
        return items

    def rs_slot(stream, dist, half):
        items = rs_items(stream)
        return items.index((dist, half)) if (dist, half) in items else None

    def rs_copy(i, stream, k):
        return remote(
            rs_send.at[i, stream, k],
            rs_recv.at[i, stream, k],
            rs_ss.at[i, stream],
            rs_rs.at[i, stream, k],
            rep=(up, down)[stream],
        )

    ready = set()

    def base(i, k, half):
        if k not in ready:
            own_copy(k).wait()
            ready.add(k)
        if (i, k) not in ready:
            sib_copy(i, k).wait_recv()
            ready.add((i, k))
        mine = own[k, half, :, i * d.CH : (i + 1) * d.CH]
        return mine.astype(F32) + sib[i, k, half].astype(F32)

    def rs_step(i, *steps):
        for k in steps:
            if k >= STEPS:
                continue
            for stream in range(2):
                dist, half = rs_items(stream)[k]
                value = base(i, dist if stream == 0 else NZ - dist, half)
                before = rs_slot(stream, dist + 1, half)
                if before is not None:
                    rs_copy(i, stream, before).wait_recv()
                    value = value + rs_recv[i, stream, before].astype(F32)
                rs_send[i, stream, k] = value.astype(BF16)
                rs_copy(i, stream, k).start()

    def ex_g(i):
        return remote(total.at[i, 1 - q], Gb.at[i, z, q], ex_ss.at[i], ex_rs.at[i], fsdp=partner)

    def rs_last(i):
        for half in range(2):
            value = base(i, 0, half)
            for stream in range(2):
                k = rs_slot(stream, 1, half)
                rs_copy(i, stream, k).wait_recv()
                value = value + rs_recv[i, stream, k].astype(F32)
            total[i, half] = (value / d.NR).astype(BF16)
        ex_g(i).start()
        Gb[i, z, q] = total[i, q]

    def aa_start(phase, send, recv):
        size = recv.shape[0] // NF
        part = recv.at[pl.ds(f * size, size)]
        sems = aa_ss.at[phase], aa_rs.at[phase]
        for to in peers:
            remote(send.at[pl.ds(to * size, size)], part, *sems, fsdp=to).start()
        recv[pl.ds(f * size, size)] = send[pl.ds(f * size, size)]

    def aa_all(phase, send, recv):
        most = pl.ds(0, recv.shape[0] // NF * (NF - 1))
        return remote(send.at[most], recv.at[most], aa_ss.at[phase], aa_rs.at[phase], fsdp=partner)

    def aa_wait(phase, send, recv):
        aa_all(phase, send, recv).wait_recv()

    def aa_done(phase, send, recv):
        aa_all(phase, send, recv).wait_send()

    def ag_items(stream):
        items = []
        for k in range(H - 1):
            items += [(k, stream), (k, 1 - stream)]
        return items + [(H - 1, stream)]

    bufs = (Gb.at[0], Gb.at[1], Rb)

    def ag_copy(a, stream, k, ahead):
        dist, half = ag_items(stream)[k]
        part = bufs[a].at[zat(-dist - ahead if stream == 0 else dist + ahead), half]
        return remote(part, part, ag_ss.at[a], ag_rs.at[a, stream, k], rep=(up, down)[stream])

    def ag_own(a):
        for k in range(2):
            for stream in range(2):
                ag_copy(a, stream, k, 0).start()

    def ag_step(a, *steps):
        for k in steps:
            if k >= STEPS:
                continue
            for stream in range(2):
                ag_copy(a, stream, k, 1).wait_recv()
                if k + 2 < STEPS:
                    ag_copy(a, stream, k + 2, 0).start()

    def ag_done(a):
        part = bufs[a].at[pl.ds(0, STEPS)]
        remote(part, part, ag_ss.at[a], ag_rs.at[a, 0, 0], rep=up).wait_send()

    wide = 2 * d.SR

    swap_roots = remote(swap_b, send_b.at[:, c], sw_ss.at[0], sw_rs.at[0], rep=sibling)

    def pick_roots():
        def go(p, carry):
            for core, to in ((1 - c, 0), (c, 1)):
                where = tab[(lax.rem(p, 2) * 2 + core) * columns + lax.div(p, 2), 0]
                for m in range(2):
                    value = recv_a[where, m]
                    if to == 0:
                        swap_b[p, m] = value
                    else:
                        send_b[p, c, m] = value
            return carry

        lax.fori_loop(0, NF, go, 0)
        swap_roots.start()

    def join_roots():
        for piece in range(NF):
            rg, cg = piece // d.CG, piece % d.CG
            cols = pl.ds(cg * d.PC, d.PC)
            for core in range(2):
                Lp[pl.ds(core * d.SR + rg * d.PR, d.PR), cols] = recv_b[piece, core, 0]
                Rs[pl.ds(core * d.SR + rg * d.PR, d.PR), cols] = recv_b[piece, core, 1]
        for dist in range(H + 1):
            at = pl.multiple_of(zat(dist) * wide, wide)
            for core in range(2):
                Rb[z, core, :, dist * wide : (dist + 1) * wide] = Rs[
                    core * d.SR : (core + 1) * d.SR, pl.ds(at, wide)
                ]

    def block(i, half):
        return Gb[i, :, half].reshape(d.BLK, d.CH)

    recv_c = (recv_c0, recv_c1)

    def swap_gram(m):
        return remote(swap_c.at[m], send_c.at[m, :, c], sw_ss.at[1 + m], sw_rs.at[1 + m], rep=sibling)

    def put_gram(m):
        value = g_s[m, 1 - c]
        for piece in range(NF):
            swap_c[m, piece] = cut(value, piece)
        swap_gram(m).start()
        value = g_s[m, c]
        for piece in range(NF):
            send_c[m, piece, c] = cut(value, piece)

    def gram_left(i):
        value = 0.0 if i == 0 else left_sum[...]
        for h in range(2):
            value = value + lax.dot_general(
                Gb[i, z, h], block(i, h), (((1,), (1,)), ((), ())), preferred_element_type=F32
            )
        if i == 0:
            left_sum[...] = value
        else:
            g_s[0] = ((1.0 - gram_decay) * value).astype(BF16).reshape(2, d.SR, d.BLK)
            put_gram(0)

    def gram_right():
        at = z * wide
        half, chain, off = at // d.HC, at % d.HC // d.CH, at % d.CH
        cols = Gb[chain, :, half, :, pl.ds(pl.multiple_of(off, wide), wide)]
        cols = cols.reshape(d.BLK, wide)
        for i in range(2):
            for h in range(2):
                both = lax.dot_general(
                    cols, block(i, h), (((0,), (0,)), ((), ())), preferred_element_type=F32
                )
                both = ((1.0 - gram_decay) * both).astype(BF16)
                first = h * d.HC + i * d.CH
                g_s[1, :, :, first : first + d.CH] = both.reshape(2, d.SR, d.CH)
        put_gram(1)

    def left_times(i):
        for h in range(2):
            first = h * d.HC + i * d.CH
            value = jnp.dot(Lp[...], block(i, h), preferred_element_type=F32).astype(BF16)
            for t in range(d.CH // wide):
                T_s[first // wide + t] = value[:, t * wide : (t + 1) * wide]

    def pick_grams(m):
        def go(o, carry):
            for s in range(d.SLOTS):
                where = jnp.maximum(tab[blocks, o * d.SLOTS + s], 0)
                send_d[m, o * d.SLOTS + s] = recv_c[m][lax.div(where, 2), lax.rem(where, 2)]
            return carry

        lax.fori_loop(0, NF, go, 0)

    def add_grams(m):
        for s in range(d.SLOTS):
            old_copy(m, s).wait()

        def go(s, carry):
            live = tab[blocks, f * d.SLOTS + s] >= 0
            for piece in range(NF):
                rg, cg = piece // d.CG, piece % d.CG
                rows, cols = pl.ds(rg * d.PR, d.PR), pl.ds(cg * d.PC, d.PC)
                added = jnp.where(live, recv_d[m, piece * d.SLOTS + s].astype(F32), 0.0)
                (new_left, new_right)[m][s, rows, cols] = (
                    gram_decay * olds[m, s, rows, cols] + added
                )
            return carry

        lax.fori_loop(0, d.SLOTS, go, 0)

    homes = (
        remote(Db.at[c, 1 - q], dir_out.at[q, c], ex_ss.at[2], ex_rs.at[2], fsdp=partner),
        remote(Db.at[1 - c, q], dir_out.at[q, c], ex_ss.at[3], ex_rs.at[3], rep=sibling),
        remote(
            Db.at[1 - c, 1 - q], dir_out.at[q, c], ex_ss.at[4], ex_rs.at[4], rep=sibling, fsdp=partner
        ),
    )

    def add_slab(dist):
        k = zat(dist)
        root = Rb[k].reshape(wide, (H + 1) * wide)
        direct = jnp.dot(T_s[k], root, preferred_element_type=F32)
        for t in range(H + 1):
            D_s[zat(dist + t)] += direct[:, t * wide : (t + 1) * wide]
        turned = jnp.concatenate([T_s[zat(dist + t)] for t in range(1, H)], axis=1)
        D_s[k] += lax.dot_general(
            turned, root[:, wide : H * wide], (((1,), (1,)), ((), ())), preferred_element_type=F32
        )

    def directions():
        for k in range(NZ):
            value = D_s[k].astype(BF16).reshape(2, d.SR, wide)
            half, at = divmod(k * wide, d.HC)
            Db[:, half, :, at : at + wide] = value
        for copy in homes:
            copy.start()
        dir_out[q, c] = Db[c, q]

    def fetch_old(s):
        for m in range(2):
            old_copy(m, s).start()

    for k in order[:3]:
        sib_copy(0, k).start()
    rs_step(0, 0)
    for k in order[3:]:
        sib_copy(0, k).start()
    rs_step(0, 1)
    for k in order:
        sib_copy(1, k).start()
    rs_step(1, 0)
    cast_root(0)
    rs_step(0, 2)
    rs_step(1, 1)
    cast_root(1)
    aa_start(0, send_a, recv_a)
    rs_step(0, 3)
    rs_step(1, 2)
    tables()
    rs_step(0, 4)
    rs_step(1, 3)
    rs_step(0, 5)
    rs_step(1, 4)
    rs_step(0, 6)
    rs_step(1, 5)
    rs_last(0)
    rs_step(1, 6)
    ex_g(0).wait_recv()
    ag_own(0)
    rs_last(1)
    ag_step(0, 0)
    ex_g(1).wait_recv()
    ag_own(1)
    ag_step(0, 1)
    aa_wait(0, send_a, recv_a)
    tab_copy.wait()
    pick_roots()
    ag_step(0, 2)
    ag_step(1, 0)
    swap_roots.wait_recv()
    aa_start(1, send_b, recv_b)
    ag_step(0, 3)
    ag_step(1, 1)
    fetch_old(0)
    ag_step(0, 4)
    ag_step(1, 2)
    fetch_old(1)
    ag_step(0, 5)
    ag_step(1, 3)
    fetch_old(2)
    ag_step(0, 6)
    gram_left(0)
    ag_step(1, 4)
    fetch_old(3)
    aa_wait(1, send_b, recv_b)
    join_roots()
    ag_own(2)
    ag_step(1, 5, 6)
    gram_left(1)
    gram_right()
    ag_step(2, 0)
    swap_gram(0).wait_recv()
    aa_start(2, send_c.at[0], recv_c0)
    swap_gram(1).wait_recv()
    aa_start(3, send_c.at[1], recv_c1)
    ag_step(2, 1)
    left_times(0)
    aa_wait(2, send_c.at[0], recv_c0)
    pick_grams(0)
    aa_start(4, send_d.at[0], recv_d.at[0])
    ag_step(2, 2)
    aa_wait(3, send_c.at[1], recv_c1)
    pick_grams(1)
    aa_start(5, send_d.at[1], recv_d.at[1])
    ag_step(2, 3)
    left_times(1)
    D_s[...] = jnp.zeros_like(D_s)
    add_slab(0)
    ag_step(2, 4)
    for dist in range(1, min(3, H)):
        add_slab(-dist)
        add_slab(dist)

    for i in range(2):
        remote(sib.at[i], sib.at[i], sib_ss.at[i], sib_rs.at[i, 0], rep=sibling).wait_send()
        for stream in range(2):
            sent = rs_send.at[i, stream]
            remote(sent, sent, rs_ss.at[i, stream], rs_rs.at[i, stream, 0], rep=up).wait_send()
        ex_g(i).wait_send()
        ag_done(i)
    aa_done(0, send_a, recv_a)
    aa_done(1, send_b, recv_b)
    swap_roots.wait_send()
    for m in range(2):
        swap_gram(m).wait_send()
        aa_done(2 + m, send_c.at[m], recv_c[m])

    ag_step(2, 5)
    for dist in range(3, H):
        add_slab(-dist)
        add_slab(dist)
    ag_step(2, 6)
    add_slab(H)
    directions()
    for m in range(2):
        aa_wait(4 + m, send_d.at[m], recv_d.at[m])
        add_grams(m)
    ag_done(2)
    for m in range(2):
        aa_done(4 + m, send_d.at[m], recv_d.at[m])
    for copy in homes:
        copy.wait()


def local(gradients, old_left, old_right, left_root, right_root, owner_plan):
    rep, fsdp = lax.axis_size("rep"), lax.axis_size("fsdp")
    _, layers, rows, home = gradients.shape
    slots = old_left.shape[0]
    d = Dims(rep, fsdp, layers, rows, home, slots)

    S, NZ, NF = d.STEPS, d.NZ, d.NF
    CR = 2 * d.SR
    piece = (d.PR, d.PC)
    vmem = lambda *shape: pltpu.VMEM(shape, BF16)
    wide = lambda *shape: pltpu.VMEM(shape, F32)
    dma = lambda *shape: pltpu.SemaphoreType.DMA(shape)
    whole = pl.BlockSpec(memory_space=pltpu.VMEM)
    away = pl.BlockSpec(memory_space=pl.ANY)
    new_left, new_right, direction = pl.pallas_call(
        functools.partial(kernel, d),
        out_shape=(
            jax.ShapeDtypeStruct(old_left.shape, F32),
            jax.ShapeDtypeStruct(old_right.shape, F32),
            jax.ShapeDtypeStruct((2, 2, d.SR, d.HC), BF16),
        ),
        in_specs=[away] * 6,
        out_specs=(whole,) * 3,
        scratch_shapes=[
            pltpu.SMEM(owner_plan.shape, jnp.int32),
            pltpu.VMEM((owner_plan.size + 8, 128), jnp.int32),
            pltpu.SMEM((owner_plan.size + 8, 128), jnp.int32),
            vmem(NZ, 2, CR, d.HC),
            vmem(2, NZ, 2, CR, d.CH),
            vmem(2, 2, S, CR, d.CH),
            vmem(2, 2, S, CR, d.CH),
            vmem(2, 2, CR, d.CH),
            wide(2, slots, d.SR, d.BLK),
            wide(2, slots, d.SR, d.BLK),
            vmem(NF * slots, 2, *piece),
            vmem(NF * slots, 2, *piece),
            vmem(NF, 2, *piece),
            vmem(NF, 2, 2, *piece),
            vmem(NF, 2, 2, *piece),
            vmem(CR, d.BLK),
            vmem(CR, d.BLK),
            vmem(2, NZ, 2, CR, d.CH),
            vmem(NZ, 2, d.SR, (d.H + 1) * CR),
            vmem(2, 2, d.SR, d.BLK),
            wide(CR, d.BLK),
            vmem(NZ, CR, CR),
            wide(NZ, CR, CR),
            vmem(2, NF, *piece),
            vmem(2, NF, 2, *piece),
            vmem(NF, 2, *piece),
            vmem(NF, 2, *piece),
            vmem(2, NF * slots, *piece),
            vmem(2, NF * slots, *piece),
            vmem(2, 2, d.SR, d.HC),
            dma(NZ),
            dma(2),
            dma(2, slots),
            pltpu.SemaphoreType.DMA,
            pltpu.SemaphoreType.DMA,
            dma(2),
            dma(2, NZ),
            dma(2, 2),
            dma(2, 2, S),
            dma(6),
            dma(6),
            dma(3),
            dma(3),
            dma(5),
            dma(5),
            dma(3),
            dma(3, 2, S),
        ],
        compiler_params=pltpu.CompilerParams(
            collective_id=0, has_side_effects=True, vmem_limit_bytes=51 * 1024 * 1024
        ),
        cost_estimate=pl.CostEstimate(
            flops=2 * 5 * 2 * d.SR * d.BLK * d.BLK,
            bytes_accessed=2 * gradients.size + 24 * left_root.size,
            transcendentals=0,
        ),
    )(
        gradients.reshape(2, 2, NZ, CR, home),
        old_left,
        old_right,
        left_root,
        right_root,
        owner_plan,
    )
    return new_left, new_right, direction.reshape(layers, d.SR, home)


def solution(mesh):
    return jax.shard_map(
        local,
        mesh=mesh,
        in_specs=(
            P("rep", None, None, "fsdp"),
            P("fsdp", "rep", None),
            P("fsdp", "rep", None),
            P("fsdp", "rep", None),
            P("fsdp", "rep", None),
            P(),
        ),
        out_specs=(P("fsdp", "rep", None), P("fsdp", "rep", None), P(None, "rep", "fsdp")),
        check_vma=False,
    )
```

time: 396 us -> 86.8 us (0.22)
  waiting for transfers between devices: 300 us -> 0 us
  Pallas kernels: 0 us -> 82.7 us
  local copies, waits for them, and re-layouts: 41.8 us -> 3.32 us
  matrix products: 35.8 us -> 0 us
  between operations: 13.9 us -> 0.65 us
    all_gather x4 -> x0, waiting for transfers between devices: 233 us -> none  [the longest x1 63.2 us: local(): row_slices = lax.all_gather(reduced, 'fsdp', axis=2, tiled=True)]
    pallas_call x0 -> x1, Pallas kernels: none -> 82.7 us  [local(): pl.pallas_call(functools.partial(kernel, d), out_shape=(jax.ShapeDtypeStr...]
    reduce_scatter x1 -> x0, waiting for transfers between devices: 66.1 us -> none  [local(): lax.psum_scatter(local_grad.astype(jnp.float32).astype(jnp.bfloat16), 're...]
    dot_general x4 -> x0, matrix products: 35.8 us -> none  [the longest x1 10.8 us: local(): jnp.einsum('sri,sci->src', left_root, lax.all_gather(transposed, 'rep', a...]
    all_gather x1 -> x0, local copies, waits for them, and re-layouts: 23.9 us -> none  [local(): everything = lax.all_gather(directions, 'fsdp', axis=0, tiled=True)]
    gather x15 -> x0, local copies, waits for them, and re-layouts: 16 us -> none
  transfers between devices with their start and end apart: 5 -> 0, of which waited for: 5 -> 0; matrix products, arithmetic and copies ran while one was open for 4% -> 0% of each run, Pallas kernels for 0% -> 0%
where the time goes in v1:
time: 86.8 us; the launch traced here: 86.7 us
  Pallas kernels  82.7 us (95%)
  local copies, waits for them, and re-layouts  3.32 us (4%)
    pallas_call x1, Pallas kernels, local(): pl.pallas_call(functools.partial(kernel, d), out_shape=(jax.ShapeDtypeStr...  82.7 us
    unnamed x5, local copies, waits for them, and re-layouts  3.32 us

profile of v1, /device:TPU:1, one launch (start us, length us, event | category | flops | bytes accessed | tf_op | source)
XLA Modules:
  0.0 86.7 jit_solution(10899627676770576516)
XLA Ops:
  0.6 0.0 copy-start
  0.6 0.7 copy-done
  1.3 82.7 %shard_map.85 = (f32[4,64,1024]{2,1,0:T(8,128)S(1)}, f32[4,64,1024]{2,1,0:T(8,128)S(1)}, bf16[2,2,64,512]{3,2,1,0:T(8,128)(2,1)S(1)}) custom-call(bf16[2,2,8,128,512]{4,3,2,1,0:T(8,128)(2,1)} %bitcast.3, f32[4,64,1024]{2,1,0:T(8,128)} %old_left.1, f32[4,64,1024]{2,1,0:T(8,128)} %old_right.1, f32[4,64,1024]{2,1,0:T(8,128)} %left_root.1, ...), custom_call_target="tpu_custom_call" | custom-call | flops 1342177280 | bytes 10485760 | tf_op jit(solution)/shard_map/pallas_call | solution.py:567
  84.0 1.0 %copy.12 = f32[4,64,1024]{2,1,0:T(8,128)} copy(f32[4,64,1024]{2,1,0:T(8,128)S(1)} %get-tuple-element.12) | data formatting | bytes 2097152
  85.0 1.0 %copy.13 = f32[4,64,1024]{2,1,0:T(8,128)} copy(f32[4,64,1024]{2,1,0:T(8,128)S(1)} %get-tuple-element.13) | data formatting | bytes 2097152
  86.0 0.7 copy.14
Async XLA Ops:
  0.6 0.7 copy-start

commit v2 on v1

--- a/solution.py
+++ b/solution.py
@@ -61,15 +61,20 @@
     Gb,
     Rb,
     g_s,
-    left_sum,
+    right_sum,
     T_s,
     D_s,
-    swap_c,
-    send_c,
-    recv_c0,
-    recv_c1,
-    send_d,
-    recv_d,
+    swap_r,
+    send_r,
+    recv_r,
+    swap_l,
+    send_l,
+    recv_l0,
+    recv_l1,
+    send_dr,
+    recv_dr,
+    send_dl,
+    recv_dl,
     Db,
     own_sem,
     root_sem,
@@ -332,46 +337,76 @@
     def block(i, half):
         return Gb[i, :, half].reshape(d.BLK, d.CH)
 
-    recv_c = (recv_c0, recv_c1)
+    near_first = [0]
+    for k in range(1, H):
+        near_first += [k, -k]
+    near_first += [H]
+    groups = near_first[: NZ // 2], near_first[NZ // 2 :]
+    swaps, sends, takes = (
+        (swap_l.at[0], swap_l.at[1], swap_r),
+        (send_l.at[0], send_l.at[1], send_r),
+        (recv_l0, recv_l1, recv_r),
+    )
+    backs = (
+        (send_dl.at[0], recv_dl.at[0]),
+        (send_dl.at[1], recv_dl.at[1]),
+        (send_dr, recv_dr),
+    )
+    span = d.BLK // 2
 
     def swap_gram(m):
-        return remote(swap_c.at[m], send_c.at[m, :, c], sw_ss.at[1 + m], sw_rs.at[1 + m], rep=sibling)
+        return remote(swaps[m], sends[m].at[:, c], sw_ss.at[1 + m], sw_rs.at[1 + m], rep=sibling)
 
     def put_gram(m):
-        value = g_s[m, 1 - c]
-        for piece in range(NF):
-            swap_c[m, piece] = cut(value, piece)
-        swap_gram(m).start()
-        value = g_s[m, c]
-        for piece in range(NF):
-            send_c[m, piece, c] = cut(value, piece)
-
-    def gram_left(i):
-        value = 0.0 if i == 0 else left_sum[...]
-        for h in range(2):
-            value = value + lax.dot_general(
-                Gb[i, z, h], block(i, h), (((1,), (1,)), ((), ())), preferred_element_type=F32
-            )
-        if i == 0:
-            left_sum[...] = value
-        else:
-            g_s[0] = ((1.0 - gram_decay) * value).astype(BF16).reshape(2, d.SR, d.BLK)
-            put_gram(0)
-
-    def gram_right():
+        width = d.PC if m == 2 else wide
+        for core, mine in ((1 - c, False), (c, True)):
+            value = g_s[1, core] if m == 2 else g_s[0, core, :, m * span : (m + 1) * span]
+            for piece in range(NF):
+                rg, cg = piece // d.CG, piece % d.CG
+                part = value[rg * d.PR : (rg + 1) * d.PR, cg * width : (cg + 1) * width]
+                if mine:
+                    sends[m][piece, c] = part
+                else:
+                    swaps[m][piece] = part
+            if not mine:
+                swap_gram(m).start()
+
+    def near(group, i, half, *cols):
+        return jnp.concatenate([Gb[i, zat(k), half, :, *cols] for k in groups[group]], axis=0)
+
+    def gram_left(group):
+        value = 0.0
+        for i in range(2):
+            for h in range(2):
+                value = value + lax.dot_general(
+                    Gb[i, z, h],
+                    near(group, i, h),
+                    (((1,), (1,)), ((), ())),
+                    preferred_element_type=F32,
+                )
+        value = ((1.0 - gram_decay) * value).astype(BF16)
+        g_s[0, :, :, group * span : (group + 1) * span] = value.reshape(2, d.SR, span)
+        put_gram(group)
+
+    def gram_right(group):
         at = z * wide
-        half, chain, off = at // d.HC, at % d.HC // d.CH, at % d.CH
-        cols = Gb[chain, :, half, :, pl.ds(pl.multiple_of(off, wide), wide)]
-        cols = cols.reshape(d.BLK, wide)
+        half, rest = lax.div(at, d.HC), lax.rem(at, d.HC)
+        chain, off = lax.div(rest, d.CH), lax.rem(rest, d.CH)
+        cols = near(group, chain, half, pl.ds(pl.multiple_of(off, wide), wide))
         for i in range(2):
             for h in range(2):
                 both = lax.dot_general(
-                    cols, block(i, h), (((0,), (0,)), ((), ())), preferred_element_type=F32
+                    cols, near(group, i, h), (((0,), (0,)), ((), ())), preferred_element_type=F32
                 )
-                both = ((1.0 - gram_decay) * both).astype(BF16)
                 first = h * d.HC + i * d.CH
-                g_s[1, :, :, first : first + d.CH] = both.reshape(2, d.SR, d.CH)
-        put_gram(1)
+                if group == 0:
+                    right_sum[:, first : first + d.CH] = both
+                else:
+                    both = both + right_sum[:, first : first + d.CH]
+                    both = ((1.0 - gram_decay) * both).astype(BF16)
+                    g_s[1, :, :, first : first + d.CH] = both.reshape(2, d.SR, d.CH)
+        if group == 1:
+            put_gram(2)
 
     def left_times(i):
         for h in range(2):
@@ -380,27 +415,43 @@
             for t in range(d.CH // wide):
                 T_s[first // wide + t] = value[:, t * wide : (t + 1) * wide]
 
-    def pick_grams(m):
+    def spread(m):
+        swap_gram(m).wait_recv()
+        aa_start(2 + m, sends[m], takes[m])
+
+    def give_back(m):
+        aa_wait(2 + m, sends[m], takes[m])
+        send, recv = backs[m]
+
         def go(o, carry):
             for s in range(d.SLOTS):
                 where = jnp.maximum(tab[blocks, o * d.SLOTS + s], 0)
-                send_d[m, o * d.SLOTS + s] = recv_c[m][lax.div(where, 2), lax.rem(where, 2)]
+                send[o * d.SLOTS + s] = takes[m][lax.div(where, 2), lax.rem(where, 2)]
             return carry
 
         lax.fori_loop(0, NF, go, 0)
+        aa_start(5 + m, send, recv)
 
     def add_grams(m):
-        for s in range(d.SLOTS):
-            old_copy(m, s).wait()
+        send, recv = backs[m]
+        aa_wait(5 + m, send, recv)
+        side = m // 2
+        if m != 1:
+            for s in range(d.SLOTS):
+                old_copy(side, s).wait()
 
         def go(s, carry):
             live = tab[blocks, f * d.SLOTS + s] >= 0
             for piece in range(NF):
                 rg, cg = piece // d.CG, piece % d.CG
-                rows, cols = pl.ds(rg * d.PR, d.PR), pl.ds(cg * d.PC, d.PC)
-                added = jnp.where(live, recv_d[m, piece * d.SLOTS + s].astype(F32), 0.0)
-                (new_left, new_right)[m][s, rows, cols] = (
-                    gram_decay * olds[m, s, rows, cols] + added
+                rows = pl.ds(rg * d.PR, d.PR)
+                if m == 2:
+                    cols = pl.ds(cg * d.PC, d.PC)
+                else:
+                    cols = pl.ds(pl.multiple_of(zat(groups[m][cg]) * wide, wide), wide)
+                added = jnp.where(live, recv[piece * d.SLOTS + s].astype(F32), 0.0)
+                (new_left, new_right)[side][s, rows, cols] = (
+                    gram_decay * olds[side, s, rows, cols] + added
                 )
             return carry
 
@@ -486,30 +537,27 @@
     ag_step(0, 5)
     ag_step(1, 3)
     fetch_old(2)
+    gram_left(0)
     ag_step(0, 6)
-    gram_left(0)
     ag_step(1, 4)
     fetch_old(3)
+    spread(0)
+    gram_right(0)
     aa_wait(1, send_b, recv_b)
     join_roots()
     ag_own(2)
+    give_back(0)
     ag_step(1, 5, 6)
+    gram_right(1)
     gram_left(1)
-    gram_right()
     ag_step(2, 0)
-    swap_gram(0).wait_recv()
-    aa_start(2, send_c.at[0], recv_c0)
-    swap_gram(1).wait_recv()
-    aa_start(3, send_c.at[1], recv_c1)
+    spread(2)
+    spread(1)
     ag_step(2, 1)
     left_times(0)
-    aa_wait(2, send_c.at[0], recv_c0)
-    pick_grams(0)
-    aa_start(4, send_d.at[0], recv_d.at[0])
+    give_back(2)
     ag_step(2, 2)
-    aa_wait(3, send_c.at[1], recv_c1)
-    pick_grams(1)
-    aa_start(5, send_d.at[1], recv_d.at[1])
+    give_back(1)
     ag_step(2, 3)
     left_times(1)
     D_s[...] = jnp.zeros_like(D_s)
@@ -529,9 +577,11 @@
     aa_done(0, send_a, recv_a)
     aa_done(1, send_b, recv_b)
     swap_roots.wait_send()
-    for m in range(2):
+    for m in range(3):
         swap_gram(m).wait_send()
-        aa_done(2 + m, send_c.at[m], recv_c[m])
+        aa_done(2 + m, sends[m], takes[m])
+    aa_done(5, *backs[0])
+    add_grams(0)
 
     ag_step(2, 5)
     for dist in range(3, H):
@@ -540,12 +590,11 @@
     ag_step(2, 6)
     add_slab(H)
     directions()
-    for m in range(2):
-        aa_wait(4 + m, send_d.at[m], recv_d.at[m])
-        add_grams(m)
+    add_grams(2)
+    add_grams(1)
     ag_done(2)
-    for m in range(2):
-        aa_done(4 + m, send_d.at[m], recv_d.at[m])
+    for m in range(1, 3):
+        aa_done(5 + m, *backs[m])
     for copy in homes:
         copy.wait()
 
@@ -597,12 +646,17 @@
             wide(CR, d.BLK),
             vmem(NZ, CR, CR),
             wide(NZ, CR, CR),
-            vmem(2, NF, *piece),
-            vmem(2, NF, 2, *piece),
+            vmem(NF, *piece),
             vmem(NF, 2, *piece),
             vmem(NF, 2, *piece),
-            vmem(2, NF * slots, *piece),
-            vmem(2, NF * slots, *piece),
+            vmem(2, NF, d.PR, CR),
+            vmem(2, NF, 2, d.PR, CR),
+            vmem(NF, 2, d.PR, CR),
+            vmem(NF, 2, d.PR, CR),
+            vmem(NF * slots, *piece),
+            vmem(NF * slots, *piece),
+            vmem(2, NF * slots, d.PR, CR),
+            vmem(2, NF * slots, d.PR, CR),
             vmem(2, 2, d.SR, d.HC),
             dma(NZ),
             dma(2),
@@ -613,10 +667,10 @@
             dma(2, NZ),
             dma(2, 2),
             dma(2, 2, S),
-            dma(6),
-            dma(6),
-            dma(3),
-            dma(3),
+            dma(8),
+            dma(8),
+            dma(4),
+            dma(4),
             dma(5),
             dma(5),
             dma(3),

time: 86.8 us -> 86.6 us (level)
  no operation moved by 1% of the time
where the time goes in v2:
time: 86.6 us; the launch traced here: 86.5 us
  Pallas kernels  82.5 us (95%)
  local copies, waits for them, and re-layouts  3.32 us (4%)
    pallas_call x1, Pallas kernels, local(): pl.pallas_call(functools.partial(kernel, d), out_shape=(jax.ShapeDtypeStr...  82.5 us
    unnamed x5, local copies, waits for them, and re-layouts  3.32 us

profile of v2, /device:TPU:1, one launch (start us, length us, event | category | flops | bytes accessed | tf_op | source)
XLA Modules:
  0.0 86.5 jit_solution(12172986421684631297)
XLA Ops:
  0.6 0.0 copy-start
  0.6 0.7 copy-done
  1.3 82.5 %shard_map.85 = (f32[4,64,1024]{2,1,0:T(8,128)S(1)}, f32[4,64,1024]{2,1,0:T(8,128)S(1)}, bf16[2,2,64,512]{3,2,1,0:T(8,128)(2,1)S(1)}) custom-call(bf16[2,2,8,128,512]{4,3,2,1,0:T(8,128)(2,1)} %bitcast.3, f32[4,64,1024]{2,1,0:T(8,128)} %old_left.1, f32[4,64,1024]{2,1,0:T(8,128)} %old_right.1, f32[4,64,1024]{2,1,0:T(8,128)} %left_root.1, ...), custom_call_target="tpu_custom_call" | custom-call | flops 1342177280 | bytes 10485760 | tf_op jit(solution)/shard_map/pallas_call | solution.py:616
  83.9 1.0 %copy.12 = f32[4,64,1024]{2,1,0:T(8,128)} copy(f32[4,64,1024]{2,1,0:T(8,128)S(1)} %get-tuple-element.12) | data formatting | bytes 2097152
  84.8 1.0 %copy.13 = f32[4,64,1024]{2,1,0:T(8,128)} copy(f32[4,64,1024]{2,1,0:T(8,128)S(1)} %get-tuple-element.13) | data formatting | bytes 2097152
  85.8 0.7 copy.14
Async XLA Ops:
  0.6 0.7 copy-start

commit v3 on v2

--- a/solution.py
+++ b/solution.py
@@ -52,7 +52,8 @@
     roots,
     olds,
     send_a,
-    recv_a,
+    recv_a0,
+    recv_a1,
     swap_b,
     send_b,
     recv_b,
@@ -139,11 +140,13 @@
         pl.semaphore_signal(barrier, inc=1, device_id=where, device_id_type=MESH)
     for peer in peers:
         pl.semaphore_signal(barrier, inc=1, device_id={"fsdp": peer}, device_id_type=MESH)
-    for k in order:
+    for k in order[:3]:
         own_copy(k).start()
-    for m in range(2):
-        root_copy(m).start()
+    root_copy(1).start()
+    root_copy(0).start()
     plan_copy.start()
+    for k in order[3:]:
+        own_copy(k).start()
     pl.semaphore_wait(barrier, NF - 1 + 4)
 
     def cut(value, piece):
@@ -156,7 +159,7 @@
         def go(s, carry):
             value = roots[m, s].astype(BF16)
             for piece in range(NF):
-                send_a[piece * d.SLOTS + s, m] = cut(value, piece)
+                send_a[m, piece * d.SLOTS + s] = cut(value, piece)
             return carry
 
         lax.fori_loop(0, d.SLOTS, go, 0)
@@ -303,30 +306,41 @@
 
     wide = 2 * d.SR
 
-    swap_roots = remote(swap_b, send_b.at[:, c], sw_ss.at[0], sw_rs.at[0], rep=sibling)
-
-    def pick_roots():
+    recv_a = (recv_a0, recv_a1)
+
+    def swap_root(m):
+        return remote(swap_b.at[m], send_b.at[m, :, c], sw_ss.at[4 + m], sw_rs.at[4 + m], rep=sibling)
+
+    def pick_root(m):
+        aa_wait(m, send_a.at[m], recv_a[m])
+
         def go(p, carry):
-            for core, to in ((1 - c, 0), (c, 1)):
+            for core, mine in ((1 - c, False), (c, True)):
                 where = tab[(lax.rem(p, 2) * 2 + core) * columns + lax.div(p, 2), 0]
-                for m in range(2):
-                    value = recv_a[where, m]
-                    if to == 0:
-                        swap_b[p, m] = value
-                    else:
-                        send_b[p, c, m] = value
+                value = recv_a[m][where]
+                if mine:
+                    send_b[m, p, c] = value
+                else:
+                    swap_b[m, p] = value
             return carry
 
         lax.fori_loop(0, NF, go, 0)
-        swap_roots.start()
-
-    def join_roots():
+        swap_root(m).start()
+
+    def pass_root(m):
+        swap_root(m).wait_recv()
+        aa_start(8 + m, send_b.at[m], recv_b.at[m])
+
+    def join_root(m):
+        aa_wait(8 + m, send_b.at[m], recv_b.at[m])
         for piece in range(NF):
             rg, cg = piece // d.CG, piece % d.CG
             cols = pl.ds(cg * d.PC, d.PC)
             for core in range(2):
-                Lp[pl.ds(core * d.SR + rg * d.PR, d.PR), cols] = recv_b[piece, core, 0]
-                Rs[pl.ds(core * d.SR + rg * d.PR, d.PR), cols] = recv_b[piece, core, 1]
+                at = core * d.SR + rg * d.PR
+                (Lp, Rs)[m][pl.ds(at, d.PR), cols] = recv_b[m, piece, core]
+        if m == 0:
+            return
         for dist in range(H + 1):
             at = pl.multiple_of(zat(dist) * wide, wide)
             for core in range(2):
@@ -498,11 +512,12 @@
     for k in order:
         sib_copy(1, k).start()
     rs_step(1, 0)
-    cast_root(0)
+    cast_root(1)
+    aa_start(1, send_a.at[1], recv_a1)
     rs_step(0, 2)
     rs_step(1, 1)
-    cast_root(1)
-    aa_start(0, send_a, recv_a)
+    cast_root(0)
+    aa_start(0, send_a.at[0], recv_a0)
     rs_step(0, 3)
     rs_step(1, 2)
     tables()
@@ -510,8 +525,11 @@
     rs_step(1, 3)
     rs_step(0, 5)
     rs_step(1, 4)
+    tab_copy.wait()
+    pick_root(1)
     rs_step(0, 6)
     rs_step(1, 5)
+    pass_root(1)
     rs_last(0)
     rs_step(1, 6)
     ex_g(0).wait_recv()
@@ -521,16 +539,13 @@
     ex_g(1).wait_recv()
     ag_own(1)
     ag_step(0, 1)
-    aa_wait(0, send_a, recv_a)
-    tab_copy.wait()
-    pick_roots()
     ag_step(0, 2)
     ag_step(1, 0)
-    swap_roots.wait_recv()
-    aa_start(1, send_b, recv_b)
+    pick_root(0)
     ag_step(0, 3)
     ag_step(1, 1)
     fetch_old(0)
+    pass_root(0)
     ag_step(0, 4)
     ag_step(1, 2)
     fetch_old(1)
@@ -543,8 +558,7 @@
     fetch_old(3)
     spread(0)
     gram_right(0)
-    aa_wait(1, send_b, recv_b)
-    join_roots()
+    join_root(1)
     ag_own(2)
     give_back(0)
     ag_step(1, 5, 6)
@@ -554,6 +568,7 @@
     spread(2)
     spread(1)
     ag_step(2, 1)
+    join_root(0)
     left_times(0)
     give_back(2)
     ag_step(2, 2)
@@ -574,9 +589,10 @@
             remote(sent, sent, rs_ss.at[i, stream], rs_rs.at[i, stream, 0], rep=up).wait_send()
         ex_g(i).wait_send()
         ag_done(i)
-    aa_done(0, send_a, recv_a)
-    aa_done(1, send_b, recv_b)
-    swap_roots.wait_send()
+    for m in range(2):
+        aa_done(m, send_a.at[m], recv_a[m])
+        aa_done(8 + m, send_b.at[m], recv_b.at[m])
+        swap_root(m).wait_send()
     for m in range(3):
         swap_gram(m).wait_send()
         aa_done(2 + m, sends[m], takes[m])
@@ -633,11 +649,12 @@
             vmem(2, 2, CR, d.CH),
             wide(2, slots, d.SR, d.BLK),
             wide(2, slots, d.SR, d.BLK),
-            vmem(NF * slots, 2, *piece),
-            vmem(NF * slots, 2, *piece),
-            vmem(NF, 2, *piece),
-            vmem(NF, 2, 2, *piece),
-            vmem(NF, 2, 2, *piece),
+            vmem(2, NF * slots, *piece),
+            vmem(NF * slots, *piece),
+            vmem(NF * slots, *piece),
+            vmem(2, NF, *piece),
+            vmem(2, NF, 2, *piece),
+            vmem(2, NF, 2, *piece),
             vmem(CR, d.BLK),
             vmem(CR, d.BLK),
             vmem(2, NZ, 2, CR, d.CH),
@@ -667,10 +684,10 @@
             dma(2, NZ),
             dma(2, 2),
             dma(2, 2, S),
-            dma(8),
-            dma(8),
-            dma(4),
-            dma(4),
+            dma(10),
+            dma(10),
+            dma(6),
+            dma(6),
             dma(5),
             dma(5),
             dma(3),

time: 86.6 us -> 86.7 us (level)
  no operation moved by 1% of the time
where the time goes in v3:
time: 86.7 us; the launch traced here: 86.6 us
  Pallas kernels  82.7 us (95%)
  local copies, waits for them, and re-layouts  3.32 us (4%)
    pallas_call x1, Pallas kernels, local(): pl.pallas_call(functools.partial(kernel, d), out_shape=(jax.ShapeDtypeStr...  82.7 us
    unnamed x5, local copies, waits for them, and re-layouts  3.32 us

profile of v3, /device:TPU:1, one launch (start us, length us, event | category | flops | bytes accessed | tf_op | source)
XLA Modules:
  0.0 86.6 jit_solution(7865468348881168376)
XLA Ops:
  0.6 0.0 copy-start
  0.6 0.7 copy-done
  1.3 82.7 %shard_map.85 = (f32[4,64,1024]{2,1,0:T(8,128)S(1)}, f32[4,64,1024]{2,1,0:T(8,128)S(1)}, bf16[2,2,64,512]{3,2,1,0:T(8,128)(2,1)S(1)}) custom-call(bf16[2,2,8,128,512]{4,3,2,1,0:T(8,128)(2,1)} %bitcast.3, f32[4,64,1024]{2,1,0:T(8,128)} %old_left.1, f32[4,64,1024]{2,1,0:T(8,128)} %old_right.1, f32[4,64,1024]{2,1,0:T(8,128)} %left_root.1, ...), custom_call_target="tpu_custom_call" | custom-call | flops 1342177280 | bytes 10485760 | tf_op jit(solution)/shard_map/pallas_call | solution.py:632
  84.0 1.0 %copy.12 = f32[4,64,1024]{2,1,0:T(8,128)} copy(f32[4,64,1024]{2,1,0:T(8,128)S(1)} %get-tuple-element.12) | data formatting | bytes 2097152
  85.0 1.0 %copy.13 = f32[4,64,1024]{2,1,0:T(8,128)} copy(f32[4,64,1024]{2,1,0:T(8,128)S(1)} %get-tuple-element.13) | data formatting | bytes 2097152
  85.9 0.7 copy.14
Async XLA Ops:
  0.6 0.7 copy-start

commit v4 on v3

--- a/solution.py
+++ b/solution.py
@@ -514,23 +514,21 @@
     rs_step(1, 0)
     cast_root(1)
     aa_start(1, send_a.at[1], recv_a1)
-    rs_step(0, 2)
-    rs_step(1, 1)
+    rs_step(0, 2, 3)
     cast_root(0)
     aa_start(0, send_a.at[0], recv_a0)
-    rs_step(0, 3)
+    rs_step(1, 1)
+    tables()
+    rs_step(0, 4, 5)
     rs_step(1, 2)
-    tables()
-    rs_step(0, 4)
+    rs_step(0, 6)
     rs_step(1, 3)
-    rs_step(0, 5)
-    rs_step(1, 4)
     tab_copy.wait()
     pick_root(1)
-    rs_step(0, 6)
+    rs_step(1, 4)
+    rs_last(0)
     rs_step(1, 5)
     pass_root(1)
-    rs_last(0)
     rs_step(1, 6)
     ex_g(0).wait_recv()
     ag_own(0)

time: 86.7 us -> 86.1 us (level)
  no operation moved by 1% of the time
where the time goes in v4:
time: 86.1 us; the launch traced here: 86 us
  Pallas kernels  82 us (95%)
  local copies, waits for them, and re-layouts  3.32 us (4%)
    pallas_call x1, Pallas kernels, local(): pl.pallas_call(functools.partial(kernel, d), out_shape=(jax.ShapeDtypeStr...  82 us
    unnamed x5, local copies, waits for them, and re-layouts  3.32 us

profile of v4, /device:TPU:1, one launch (start us, length us, event | category | flops | bytes accessed | tf_op | source)
XLA Modules:
  0.0 86.0 jit_solution(15011550511476185261)
XLA Ops:
  0.6 0.0 copy-start
  0.6 0.7 copy-done
  1.3 82.0 %shard_map.85 = (f32[4,64,1024]{2,1,0:T(8,128)S(1)}, f32[4,64,1024]{2,1,0:T(8,128)S(1)}, bf16[2,2,64,512]{3,2,1,0:T(8,128)(2,1)S(1)}) custom-call(bf16[2,2,8,128,512]{4,3,2,1,0:T(8,128)(2,1)} %bitcast.3, f32[4,64,1024]{2,1,0:T(8,128)} %old_left.1, f32[4,64,1024]{2,1,0:T(8,128)} %old_right.1, f32[4,64,1024]{2,1,0:T(8,128)} %left_root.1, ...), custom_call_target="tpu_custom_call" | custom-call | flops 1342177280 | bytes 10485760 | tf_op jit(solution)/shard_map/pallas_call | solution.py:630
  83.3 1.0 %copy.12 = f32[4,64,1024]{2,1,0:T(8,128)} copy(f32[4,64,1024]{2,1,0:T(8,128)S(1)} %get-tuple-element.12) | data formatting | bytes 2097152
  84.3 1.0 %copy.13 = f32[4,64,1024]{2,1,0:T(8,128)} copy(f32[4,64,1024]{2,1,0:T(8,128)S(1)} %get-tuple-element.13) | data formatting | bytes 2097152
  85.3 0.7 copy.14
Async XLA Ops:
  0.6 0.7 copy-start

commit v5 on v4

--- a/solution.py
+++ b/solution.py
@@ -519,6 +519,7 @@
     aa_start(0, send_a.at[0], recv_a0)
     rs_step(1, 1)
     tables()
+    D_s[...] = jnp.zeros_like(D_s)
     rs_step(0, 4, 5)
     rs_step(1, 2)
     rs_step(0, 6)
@@ -567,15 +568,14 @@
     spread(1)
     ag_step(2, 1)
     join_root(0)
+    ag_step(2, 2)
+    give_back(2)
+    ag_step(2, 3)
+    give_back(1)
+    ag_step(2, 4)
     left_times(0)
-    give_back(2)
-    ag_step(2, 2)
-    give_back(1)
-    ag_step(2, 3)
     left_times(1)
-    D_s[...] = jnp.zeros_like(D_s)
     add_slab(0)
-    ag_step(2, 4)
     for dist in range(1, min(3, H)):
         add_slab(-dist)
         add_slab(dist)

time: 86.1 us -> 86.1 us (level)
  no operation moved by 1% of the time
where the time goes in v5:
time: 86.1 us; the launch traced here: 86 us
  Pallas kernels  82 us (95%)
  local copies, waits for them, and re-layouts  3.32 us (4%)
    pallas_call x1, Pallas kernels, local(): pl.pallas_call(functools.partial(kernel, d), out_shape=(jax.ShapeDtypeStr...  82 us
    unnamed x5, local copies, waits for them, and re-layouts  3.32 us

profile of v5, /device:TPU:1, one launch (start us, length us, event | category | flops | bytes accessed | tf_op | source)
XLA Modules:
  0.0 86.0 jit_solution(6128416005329755292)
XLA Ops:
  0.6 0.0 copy-start
  0.6 0.7 copy-done
  1.3 82.0 %shard_map.85 = (f32[4,64,1024]{2,1,0:T(8,128)S(1)}, f32[4,64,1024]{2,1,0:T(8,128)S(1)}, bf16[2,2,64,512]{3,2,1,0:T(8,128)(2,1)S(1)}) custom-call(bf16[2,2,8,128,512]{4,3,2,1,0:T(8,128)(2,1)} %bitcast.3, f32[4,64,1024]{2,1,0:T(8,128)} %old_left.1, f32[4,64,1024]{2,1,0:T(8,128)} %old_right.1, f32[4,64,1024]{2,1,0:T(8,128)} %left_root.1, ...), custom_call_target="tpu_custom_call" | custom-call | flops 1342177280 | bytes 10485760 | tf_op jit(solution)/shard_map/pallas_call | solution.py:630
  83.3 1.0 %copy.12 = f32[4,64,1024]{2,1,0:T(8,128)} copy(f32[4,64,1024]{2,1,0:T(8,128)S(1)} %get-tuple-element.12) | data formatting | bytes 2097152
  84.3 1.0 %copy.13 = f32[4,64,1024]{2,1,0:T(8,128)} copy(f32[4,64,1024]{2,1,0:T(8,128)S(1)} %get-tuple-element.13) | data formatting | bytes 2097152
  85.3 0.7 copy.14
Async XLA Ops:
  0.6 0.7 copy-start
